TPU v7x, 32 devices: a whole 2x2x4 slice. The times are simulated.
32 devices in a mesh: seq: 8 (over y, x, core), head: 4 (over z).
Axes of the slice: x: 2, y: 2, z: 4, core: 2. Of those that a mesh axis runs over, the one named last changes fastest.
Arguments:
- tokens: bfloat16 [8192, 2048], P(('seq', 'head')), may hold values from -6 to 6
- lengths: int32 [16], replicated, may hold values from 1 to 4096, 8192 in all
- w_query: bfloat16 [2048, 2048], P(None, 'head'), may hold values from -0.125 to 0.125
- w_key: bfloat16 [2048, 2048], P(None, 'head'), may hold values from -0.125 to 0.125
- w_value: bfloat16 [2048, 2048], P(None, 'head'), may hold values from -0.125 to 0.125
- w_gate: bfloat16 [2048, 2048], P(None, 'head'), may hold values from -0.125 to 0.125
- w_forget: bfloat16 [2048, 2048], P(None, 'head'), may hold values from -0.125 to 0.125
- decay_rate: float32 [2048], P('head'), may hold values from 6.1035157e-06 to 0.04
- w_out: bfloat16 [2048, 2048], P('head'), may hold values from -0.125 to 0.125
Outputs:
- output: bfloat16 [8192, 2048], P(('seq', 'head'))
- states: float32 [8, 16, 128, 128], P('seq', 'head')
Inputs may be any that keep to these rules, and one draw needn't show every extreme that they name: lengths of the prompts in stream order; they sum to 8192 and the longest is exactly 4096.
All inputs are finite; a program needn't handle non-finite values.
Results may differ from a plain program's by a relative error of at most 0.0085.
Values may be sent and summed in bfloat16 or wider, within the bound.
A program may use at most 128 MiB of HBM per device.

v0:
```python
import jax
import jax.numpy as jnp
from jax import lax
from jax.sharding import PartitionSpec as P

DK = 128
SPAN = 128


def passed_along(shard, axis, by):
    devices = lax.axis_size(axis)
    pairs = [(i, i + by) for i in range(devices) if 0 <= i + by < devices]
    return lax.ppermute(shard, axis, pairs)


def span_pass(carried, inputs):
    held_state, prev_doc = carried
    queries, key_rows, value_rows, log_decay, doc_ids = inputs
    cumulative = jnp.cumsum(log_decay, axis=0)
    scaled_q = queries.astype(jnp.float32) * jnp.exp(cumulative)
    scaled_k = key_rows.astype(jnp.float32) * jnp.exp(-cumulative)
    scores = jnp.einsum("thc,shc->hts", scaled_q, scaled_k, precision=lax.Precision.HIGHEST)
    length = doc_ids.shape[0]
    lower_tri = jnp.arange(length)[:, None] >= jnp.arange(length)[None, :]
    same_doc = (doc_ids[:, None] == doc_ids[None, :]) & lower_tri
    scores = jnp.where(same_doc[None], scores, 0.0)
    within = jnp.einsum(
        "hts,shd->thd",
        scores,
        value_rows,
        precision=lax.Precision.HIGHEST,
        preferred_element_type=jnp.float32,
    )
    carry_mask = (doc_ids == prev_doc).astype(jnp.float32)
    from_state = jnp.einsum("thc,hcd->thd", scaled_q, held_state, precision=lax.Precision.HIGHEST)
    last_doc = doc_ids[-1]
    end_decay = jnp.exp(cumulative[-1])
    weighted = scaled_k * end_decay[None] * (doc_ids == last_doc).astype(jnp.float32)[:, None, None]
    keep_old = end_decay * (last_doc == prev_doc).astype(jnp.float32)
    new_state = held_state * keep_old[:, :, None] + jnp.einsum(
        "shc,shd->hcd",
        weighted,
        value_rows,
        precision=lax.Precision.HIGHEST,
        preferred_element_type=jnp.float32,
    )
    return ((new_state, last_doc), within + from_state * carry_mask[:, None, None])


def local(tokens, lengths, w_query, w_key, w_value, w_gate, w_forget, decay_rate, w_out):
    tokens_f = tokens.astype(jnp.float32)
    normed = (
        tokens_f * lax.rsqrt(jnp.mean(tokens_f * tokens_f, axis=-1, keepdims=True) + 1e-05)
    ).astype(jnp.bfloat16)
    width = w_query.shape[1]
    group_heads = width // DK
    matrices = (w_query, w_key, w_value, w_gate, w_forget)
    piece = lax.all_gather(normed, "head", axis=0, tiled=True)
    projected = jnp.concatenate(
        [jnp.dot(piece, matrix, preferred_element_type=jnp.float32) for matrix in matrices], axis=1
    )
    seg_len = projected.shape[0]
    queries = projected[:, :width].astype(jnp.bfloat16)
    key_rows = projected[:, width : 2 * width].astype(jnp.bfloat16)
    value_rows = projected[:, 2 * width : 3 * width].astype(jnp.bfloat16)
    gate_rows = projected[:, 3 * width : 4 * width].astype(jnp.bfloat16)
    queries, key_rows, value_rows, gate_rows = lax.optimization_barrier(
        (queries, key_rows, value_rows, gate_rows)
    )
    forget_logit = projected[:, 4 * width :]
    log_decay = -decay_rate[None, :] * jax.nn.softplus(forget_logit)
    seg_start = lax.axis_index("seq") * seg_len
    positions = seg_start - 1 + jnp.arange(seg_len + 1, dtype=jnp.int32)
    doc_ends = jnp.cumsum(lengths)
    starts = doc_ends - lengths
    doc_ids = jnp.sum((starts[None, :] <= positions[:, None]).astype(jnp.int32), axis=1) - 1
    prev_doc = doc_ids[0]
    own_docs = doc_ids[1:]
    spans = seg_len // SPAN

    def blocks(array):
        return array.reshape(spans, SPAN, group_heads, DK)

    inputs = (
        blocks(queries),
        blocks(key_rows),
        blocks(value_rows),
        blocks(log_decay),
        own_docs.reshape(spans, SPAN),
    )
    start_state = jnp.zeros((group_heads, DK, DK), jnp.float32)
    (local_state, _), within = lax.scan(span_pass, (start_state, prev_doc), inputs)
    within = within.reshape(seg_len, group_heads, DK)
    total_decay = jnp.cumsum(log_decay, axis=0)
    seg_decay = (jnp.exp(total_decay[-1]) * (own_docs[-1] == prev_doc).astype(jnp.float32)).reshape(
        group_heads, DK
    )

    def relay(turn, inbound):
        return passed_along(
            (seg_decay[:, :, None] * inbound + local_state).astype(jnp.bfloat16), "seq", 1
        ).astype(jnp.float32)

    incoming = lax.fori_loop(0, lax.axis_size("seq") - 1, relay, jnp.zeros_like(local_state))
    carry_mask = (own_docs == prev_doc).astype(jnp.float32)
    carried_q = (queries.astype(jnp.float32) * jnp.exp(total_decay)).reshape(
        seg_len, group_heads, DK
    ) * carry_mask[:, None, None]
    from_state = jnp.einsum("thc,hcd->thd", carried_q, incoming, precision=lax.Precision.HIGHEST)
    mixed = within + from_state
    inverse = lax.rsqrt(jnp.mean(mixed * mixed, axis=-1, keepdims=True) + 1e-05)
    gate_f = jax.nn.silu(gate_rows.astype(jnp.float32)).reshape(seg_len, group_heads, DK)
    gated = (mixed * inverse * gate_f).astype(jnp.bfloat16).reshape(seg_len, width)
    summed = lax.psum_scatter(
        jnp.dot(gated, w_out, preferred_element_type=jnp.float32).astype(jnp.bfloat16),
        "head",
        scatter_dimension=0,
        tiled=True,
    ).astype(jnp.float32)
    output = (tokens_f + summed).astype(jnp.bfloat16)
    end_state = seg_decay[:, :, None] * incoming + local_state
    return (output, end_state[None])


def solution(mesh):
    in_specs = (
        P(("seq", "head"), None),
        P(),
        P(None, "head"),
        P(None, "head"),
        P(None, "head"),
        P(None, "head"),
        P(None, "head"),
        P("head"),
        P("head", None),
    )
    out_specs = (P(("seq", "head"), None), P("seq", "head", None, None))
    return jax.shard_map(local, mesh=mesh, in_specs=in_specs, out_specs=out_specs, check_vma=False)
```

profile of v0, /device:TPU:23, one launch (start us, length us, event | category | flops | bytes accessed | tf_op | source)
XLA Modules:
  0.0 420.1 jit_solution(1514540685137676414)
XLA Ops:
  7.2 1.6 fusion.21
  8.9 2.4 fusion.22
  14.3 77.5 %all-gather.2.cloned.1.call-done = bf16[1024,2048]{1,0:T(8,128)(2,1)} async-done(((bf16[256,2048]{1,0:T(8,128)(2,1)}), bf16[1024,2048]{1,0:T(8,128)(2,1)}) %all-gather.2.cloned.1.call-update) | async-done | bytes 4194320 | tf_op jit(solution)/shard_map/all_gather | solution.py:58
  91.8 8.0 %fusion.24 = (f32[1024,512]{1,0:T(8,128)}, f32[1024,512]{1,0:T(8,128)}) fusion(f32[512]{0:T(512)S(1)} %neg.18, bf16[1024,2048]{1,0:T(8,128)(2,1)} %all-gather.2.cloned.1.call-done, bf16[2048,512]{1,0:T(8,128)(2,1)} %param.19), kind=kOutput, calls=%fused_computation.48 | convolution fusion | flops 2151153664 | bytes 10487808 | tf_op jit(solution)/shard_map/dot_general | solution.py:60
  99.8 2.9 reshape.177
  102.8 6.3 %convolution_convert_fusion.1 = bf16[1024,512]{1,0:T(8,128)(2,1)} fusion(bf16[1024,2048]{1,0:T(8,128)(2,1)} %all-gather.2.cloned.1.call-done, bf16[2048,512]{1,0:T(8,128)(2,1)} %param.18), kind=kOutput, calls=%fused_computation.65 | convolution fusion | flops 2148007936 | bytes 7340032 | tf_op jit(solution)/shard_map/dot_general | solution.py:60
  109.1 3.3 convolution_convert_fusion.2
  112.4 3.3 convolution_convert_fusion.3
  115.7 3.3 convolution_convert_fusion.4
  119.0 2.2 reshape.179
  121.2 2.1 reshape.180
  123.4 2.2 reshape.181
  125.5 2.7 fusion.25
  128.3 1.3 fusion.32
  129.6 1.3 copy-done.1
  131.0 1.8 broadcast_add_fusion
  132.8 1.2 copy.45
  134.1 1.7 multiply_bitcast_fusion.1
  136.1 1.9 convert_multiply_fusion.4
  138.0 2.9 copy.52
  140.9 128.1 %while.26 = (s32[]{:T(128)}, f32[4,128,128]{2,1,0:T(8,128)S(1)}, s32[]{:T(128)}, f32[8,128,4,128]{1,0,3,2:T(8,128)}, f32[8,128,4,128]{3,2,1,0:T(4,128)}, /*index...) while((s32[]{:T(128)}, f32[4,128,128]{2,1,0:T(8,128)S(1)}, ...), condition=%wide.region_5.6_spmd.clone, body=%wide.region_3.5_spmd.clone.sunk | while | flops 411943936 | bytes 6076606 | solution.py:92
  144.3 1.1 fusion.69
  145.4 1.2 multiply_multiply_fusion.2
  148.7 8.2 %dynamic_update_slice.6 = f32[8,128,4,128]{1,0,3,2:T(8,128)} dynamic-update-slice(f32[8,128,4,128]{1,0,3,2:T(8,128)} %get-tuple-element.302, f32[1,128,4,128]{1,0,3,2:T(1,128)S(1)} %bitcast.121, s32[]{:T(128)S(6)} %copy.99, s32[]{:T(128)} %constant.39.clone.1..sunk, s32[]{:T(128)} %constant.39.clone.1..sunk, s32[]{:T(128)} %constant.39.clone.1..sunk) | dynamic-update-slice | bytes 524292 | tf_op jit(solution)/shard_map/while/body/jit(dynamic_update_index_in_dim)/dynamic_update_slice | solution.py:92
  160.3 1.1 fusion.69
  161.4 1.2 multiply_multiply_fusion.2
  164.7 8.2 %dynamic_update_slice.6 = f32[8,128,4,128]{1,0,3,2:T(8,128)} dynamic-update-slice(f32[8,128,4,128]{1,0,3,2:T(8,128)} %get-tuple-element.302, f32[1,128,4,128]{1,0,3,2:T(1,128)S(1)} %bitcast.121, s32[]{:T(128)S(6)} %copy.99, s32[]{:T(128)} %constant.39.clone.1..sunk, s32[]{:T(128)} %constant.39.clone.1..sunk, s32[]{:T(128)} %constant.39.clone.1..sunk) | dynamic-update-slice | bytes 524292 | tf_op jit(solution)/shard_map/while/body/jit(dynamic_update_index_in_dim)/dynamic_update_slice | solution.py:92
  176.3 1.1 fusion.69
  177.4 1.2 multiply_multiply_fusion.2
  180.7 8.2 %dynamic_update_slice.6 = f32[8,128,4,128]{1,0,3,2:T(8,128)} dynamic-update-slice(f32[8,128,4,128]{1,0,3,2:T(8,128)} %get-tuple-element.302, f32[1,128,4,128]{1,0,3,2:T(1,128)S(1)} %bitcast.121, s32[]{:T(128)S(6)} %copy.99, s32[]{:T(128)} %constant.39.clone.1..sunk, s32[]{:T(128)} %constant.39.clone.1..sunk, s32[]{:T(128)} %constant.39.clone.1..sunk) | dynamic-update-slice | bytes 524292 | tf_op jit(solution)/shard_map/while/body/jit(dynamic_update_index_in_dim)/dynamic_update_slice | solution.py:92
  192.3 1.1 fusion.69
  193.4 1.2 multiply_multiply_fusion.2
  196.7 8.2 %dynamic_update_slice.6 = f32[8,128,4,128]{1,0,3,2:T(8,128)} dynamic-update-slice(f32[8,128,4,128]{1,0,3,2:T(8,128)} %get-tuple-element.302, f32[1,128,4,128]{1,0,3,2:T(1,128)S(1)} %bitcast.121, s32[]{:T(128)S(6)} %copy.99, s32[]{:T(128)} %constant.39.clone.1..sunk, s32[]{:T(128)} %constant.39.clone.1..sunk, s32[]{:T(128)} %constant.39.clone.1..sunk) | dynamic-update-slice | bytes 524292 | tf_op jit(solution)/shard_map/while/body/jit(dynamic_update_index_in_dim)/dynamic_update_slice | solution.py:92
  208.3 1.1 fusion.69
  209.4 1.2 multiply_multiply_fusion.2
  212.7 8.2 %dynamic_update_slice.6 = f32[8,128,4,128]{1,0,3,2:T(8,128)} dynamic-update-slice(f32[8,128,4,128]{1,0,3,2:T(8,128)} %get-tuple-element.302, f32[1,128,4,128]{1,0,3,2:T(1,128)S(1)} %bitcast.121, s32[]{:T(128)S(6)} %copy.99, s32[]{:T(128)} %constant.39.clone.1..sunk, s32[]{:T(128)} %constant.39.clone.1..sunk, s32[]{:T(128)} %constant.39.clone.1..sunk) | dynamic-update-slice | bytes 524292 | tf_op jit(solution)/shard_map/while/body/jit(dynamic_update_index_in_dim)/dynamic_update_slice | solution.py:92
  224.3 1.1 fusion.69
  225.4 1.2 multiply_multiply_fusion.2
  228.7 8.2 %dynamic_update_slice.6 = f32[8,128,4,128]{1,0,3,2:T(8,128)} dynamic-update-slice(f32[8,128,4,128]{1,0,3,2:T(8,128)} %get-tuple-element.302, f32[1,128,4,128]{1,0,3,2:T(1,128)S(1)} %bitcast.121, s32[]{:T(128)S(6)} %copy.99, s32[]{:T(128)} %constant.39.clone.1..sunk, s32[]{:T(128)} %constant.39.clone.1..sunk, s32[]{:T(128)} %constant.39.clone.1..sunk) | dynamic-update-slice | bytes 524292 | tf_op jit(solution)/shard_map/while/body/jit(dynamic_update_index_in_dim)/dynamic_update_slice | solution.py:92
  240.3 1.1 fusion.69
  241.4 1.2 multiply_multiply_fusion.2
  244.7 8.2 %dynamic_update_slice.6 = f32[8,128,4,128]{1,0,3,2:T(8,128)} dynamic-update-slice(f32[8,128,4,128]{1,0,3,2:T(8,128)} %get-tuple-element.302, f32[1,128,4,128]{1,0,3,2:T(1,128)S(1)} %bitcast.121, s32[]{:T(128)S(6)} %copy.99, s32[]{:T(128)} %constant.39.clone.1..sunk, s32[]{:T(128)} %constant.39.clone.1..sunk, s32[]{:T(128)} %constant.39.clone.1..sunk) | dynamic-update-slice | bytes 524292 | tf_op jit(solution)/shard_map/while/body/jit(dynamic_update_index_in_dim)/dynamic_update_slice | solution.py:92
  257.4 1.2 multiply_multiply_fusion.2
  260.8 8.2 %dynamic_update_slice.6 = f32[8,128,4,128]{1,0,3,2:T(8,128)} dynamic-update-slice(f32[8,128,4,128]{1,0,3,2:T(8,128)} %get-tuple-element.302, f32[1,128,4,128]{1,0,3,2:T(1,128)S(1)} %bitcast.121, s32[]{:T(128)S(6)} %copy.99, s32[]{:T(128)} %constant.39.clone.1..sunk, s32[]{:T(128)} %constant.39.clone.1..sunk, s32[]{:T(128)} %constant.39.clone.1..sunk) | dynamic-update-slice | bytes 524292 | tf_op jit(solution)/shard_map/while/body/jit(dynamic_update_index_in_dim)/dynamic_update_slice | solution.py:92
  269.0 2.7 reshape.182
  272.4 42.4 %while.27 = (s32[]{:T(128)}, f32[4,128,128]{2,1,0:T(8,128)S(1)}, f32[512]{0:T(512)S(1)}, f32[4,128,128]{2,1,0:T(8,128)S(1)}, s32[]{:T(128)}, /*index=5*/s32[]{:T(128)}) while((s32[]{:T(128)}, f32[4,128,128]{2,1,0:T(8,128)S(1)}, f32[512]{0:T(512)S(1)}, f32[4,128,128]{2,1,0:T(8,128)S(1)}, s32[]{:T(128)}, /*index=5*/s32[]{:T(128)}) %tuple.71), condition=%wide.region_9.10_spmd.clone, body=%wide.region_8.9_spmd.clone.sunk | while | flops 327683 | bytes 1575031 | solution.py:104
  272.6 1.3 collective-permute-start
  273.9 2.1 collective-permute-done
  276.2 1.3 collective-permute-start
  277.5 5.0 %collective-permute-done = bf16[4,128,128]{2,1,0:T(8,128)(2,1)S(1)} collective-permute-done((bf16[4,128,128]{2,1,0:T(8,128)(2,1)S(1)}, bf16[4,128,128]{2,1,0:T(8,128)(2,1)S(1)}, u32[]{:S(2)}, u32[]{:S(2)}) %collective-permute-start) | collective-permute-done | bytes 131104 | tf_op jit(solution)/shard_map/while/body/eval_jaxpr/ppermute | solution.py:13
  282.6 1.3 collective-permute-start
  283.9 5.0 %collective-permute-done = bf16[4,128,128]{2,1,0:T(8,128)(2,1)S(1)} collective-permute-done((bf16[4,128,128]{2,1,0:T(8,128)(2,1)S(1)}, bf16[4,128,128]{2,1,0:T(8,128)(2,1)S(1)}, u32[]{:S(2)}, u32[]{:S(2)}) %collective-permute-start) | collective-permute-done | bytes 131104 | tf_op jit(solution)/shard_map/while/body/eval_jaxpr/ppermute | solution.py:13
  289.1 1.3 collective-permute-start
  290.4 5.0 %collective-permute-done = bf16[4,128,128]{2,1,0:T(8,128)(2,1)S(1)} collective-permute-done((bf16[4,128,128]{2,1,0:T(8,128)(2,1)S(1)}, bf16[4,128,128]{2,1,0:T(8,128)(2,1)S(1)}, u32[]{:S(2)}, u32[]{:S(2)}) %collective-permute-start) | collective-permute-done | bytes 131104 | tf_op jit(solution)/shard_map/while/body/eval_jaxpr/ppermute | solution.py:13
  295.6 1.3 collective-permute-start
  296.9 5.0 %collective-permute-done = bf16[4,128,128]{2,1,0:T(8,128)(2,1)S(1)} collective-permute-done((bf16[4,128,128]{2,1,0:T(8,128)(2,1)S(1)}, bf16[4,128,128]{2,1,0:T(8,128)(2,1)S(1)}, u32[]{:S(2)}, u32[]{:S(2)}) %collective-permute-start) | collective-permute-done | bytes 131104 | tf_op jit(solution)/shard_map/while/body/eval_jaxpr/ppermute | solution.py:13
  302.0 1.3 collective-permute-start
  303.3 5.0 %collective-permute-done = bf16[4,128,128]{2,1,0:T(8,128)(2,1)S(1)} collective-permute-done((bf16[4,128,128]{2,1,0:T(8,128)(2,1)S(1)}, bf16[4,128,128]{2,1,0:T(8,128)(2,1)S(1)}, u32[]{:S(2)}, u32[]{:S(2)}) %collective-permute-start) | collective-permute-done | bytes 131104 | tf_op jit(solution)/shard_map/while/body/eval_jaxpr/ppermute | solution.py:13
  308.5 1.3 collective-permute-start
  309.8 5.0 %collective-permute-done = bf16[4,128,128]{2,1,0:T(8,128)(2,1)S(1)} collective-permute-done((bf16[4,128,128]{2,1,0:T(8,128)(2,1)S(1)}, bf16[4,128,128]{2,1,0:T(8,128)(2,1)S(1)}, u32[]{:S(2)}, u32[]{:S(2)}) %collective-permute-start) | collective-permute-done | bytes 131104 | tf_op jit(solution)/shard_map/while/body/eval_jaxpr/ppermute | solution.py:13
  314.8 4.8 %multiply_reduce_fusion = (f32[1024,4]{0,1:T(4,128)S(1)}, f32[1024,4,128]{0,2,1:T(8,128)S(1)}) fusion(f32[1024,4,128]{0,2,1:T(8,128)} %reshape.182, f32[4,128,128]{2,1,0:T(8,128)S(1)} %get-tuple-element.81, f32[128,4,8,128]{3,2,1,0:T(8,128)} %multiply_bitcast_fusion.1, f32[1024]{0:T(1024)S(1)} %compare_convert_fusion.2), kind=kOutput, calls=%fused_computation.63 | convolution fusion | flops 807399424 | bytes 6574080 | tf_op jit(solution)/shard_map/thc,hcd->thd/dot_general | solution.py:109
  320.2 4.3 %convolution_convert_fusion = bf16[1024,2048]{1,0:T(8,128)(2,1)} fusion(bf16[1024,512]{0,1:T(8,128)(2,1)S(1)} %bitcast.125, bf16[512,2048]{1,0:T(8,128)(2,1)S(1)} %copy-done), kind=kOutput, calls=%fused_computation.36 | convolution fusion | flops 2149580800 | bytes 7340032 | tf_op jit(solution)/shard_map/dot_general | solution.py:115
  325.4 84.9 %reduce-scatter.2.cloned.1.call-done = bf16[256,2048]{1,0:T(8,128)(2,1)} async-done(((bf16[1024,2048]{1,0:T(8,128)(2,1)}), bf16[256,2048]{1,0:T(8,128)(2,1)}) %reduce-scatter.2.cloned.1.call-update) | async-done | bytes 1048592 | tf_op jit(solution)/shard_map/reduce_scatter | solution.py:114
  410.3 2.9 fusion.23
  (144 shorter events, 40.8 us)
Async XLA Ops:
  7.2 313.0 %copy-start = (bf16[512,2048]{1,0:T(8,128)(2,1)S(1)}, bf16[512,2048]{1,0:T(8,128)(2,1)}, u32[]{:S(2)}) copy-start(bf16[512,2048]{1,0:T(8,128)(2,1)} %param.21) | copy-start | bytes 6291460
  7.2 4.3 %copy-start.6 = (f32[512]{0:T(512)S(1)}, f32[512]{0:T(512)}, u32[]{:S(2)}) copy-start(f32[512]{0:T(512)} %param.20) | copy-start | bytes 6148
  7.2 4.3 %copy-start.7 = (s32[16]{0:T(128)S(1)}, s32[16]{0:T(128)}, u32[]{:S(2)}) copy-start(s32[16]{0:T(128)} %param.14) | copy-start | bytes 196
  7.2 84.6 %all-gather.2.cloned.1.call-start = ((), (), s32[]{:S(2)}) async-start(), calls=%async_computation.1 | async-start | bytes 5242880 | tf_op jit(solution)/shard_map/all_gather | solution.py:58
  11.4 399.0 %reduce-scatter.2.cloned.1.call-start = ((), (), s32[]{:S(2)}) async-start(), calls=%async_computation.2 | async-start | bytes 5242880 | tf_op jit(solution)/shard_map/reduce_scatter | solution.py:114
  102.8 6.3 %copy-start.8 = (bf16[1024,2048]{1,0:T(8,128)(2,1)S(1)}, bf16[1024,2048]{1,0:T(8,128)(2,1)}, u32[]{:S(2)}) copy-start(bf16[1024,2048]{1,0:T(8,128)(2,1)} %all-gather.2.cloned.1.call-done) | copy-start | bytes 12582916
  102.8 6.3 %copy-start.9 = (bf16[2048,512]{1,0:T(8,128)(2,1)S(1)}, bf16[2048,512]{1,0:T(8,128)(2,1)}, u32[]{:S(2)}) copy-start(bf16[2048,512]{1,0:T(8,128)(2,1)} %param.17) | copy-start | bytes 6291460
  109.1 3.3 copy-start.10
  112.4 3.3 copy-start.11
  129.6 1.3 copy-start.1
  132.8 1.2 copy-start.4
  134.0 2.1 copy-start.2
  134.0 2.1 copy-start.5
  272.6 3.4 collective-permute-start
  276.2 6.3 %collective-permute-start = (bf16[4,128,128]{2,1,0:T(8,128)(2,1)S(1)}, bf16[4,128,128]{2,1,0:T(8,128)(2,1)S(1)}, u32[]{:S(2)}, u32[]{:S(2)}) collective-permute-start(bf16[4,128,128]{2,1,0:T(8,128)(2,1)S(1)} %fusion.72), channel_id=1, source_target_pairs={{0,4},{4,8},{8,12},{12,16},{16,20},{20,24},{24,28},{1,5},{5,9},{9,... | collective-permute-start | bytes 393224 | tf_op jit(solution)/shard_map/while/body/eval_jaxpr/ppermute | solution.py:13
  282.6 6.3 %collective-permute-start = (bf16[4,128,128]{2,1,0:T(8,128)(2,1)S(1)}, bf16[4,128,128]{2,1,0:T(8,128)(2,1)S(1)}, u32[]{:S(2)}, u32[]{:S(2)}) collective-permute-start(bf16[4,128,128]{2,1,0:T(8,128)(2,1)S(1)} %fusion.72), channel_id=1, source_target_pairs={{0,4},{4,8},{8,12},{12,16},{16,20},{20,24},{24,28},{1,5},{5,9},{9,... | collective-permute-start | bytes 393224 | tf_op jit(solution)/shard_map/while/body/eval_jaxpr/ppermute | solution.py:13
  289.1 6.3 %collective-permute-start = (bf16[4,128,128]{2,1,0:T(8,128)(2,1)S(1)}, bf16[4,128,128]{2,1,0:T(8,128)(2,1)S(1)}, u32[]{:S(2)}, u32[]{:S(2)}) collective-permute-start(bf16[4,128,128]{2,1,0:T(8,128)(2,1)S(1)} %fusion.72), channel_id=1, source_target_pairs={{0,4},{4,8},{8,12},{12,16},{16,20},{20,24},{24,28},{1,5},{5,9},{9,... | collective-permute-start | bytes 393224 | tf_op jit(solution)/shard_map/while/body/eval_jaxpr/ppermute | solution.py:13
  295.6 6.3 %collective-permute-start = (bf16[4,128,128]{2,1,0:T(8,128)(2,1)S(1)}, bf16[4,128,128]{2,1,0:T(8,128)(2,1)S(1)}, u32[]{:S(2)}, u32[]{:S(2)}) collective-permute-start(bf16[4,128,128]{2,1,0:T(8,128)(2,1)S(1)} %fusion.72), channel_id=1, source_target_pairs={{0,4},{4,8},{8,12},{12,16},{16,20},{20,24},{24,28},{1,5},{5,9},{9,... | collective-permute-start | bytes 393224 | tf_op jit(solution)/shard_map/while/body/eval_jaxpr/ppermute | solution.py:13
  302.0 6.3 %collective-permute-start = (bf16[4,128,128]{2,1,0:T(8,128)(2,1)S(1)}, bf16[4,128,128]{2,1,0:T(8,128)(2,1)S(1)}, u32[]{:S(2)}, u32[]{:S(2)}) collective-permute-start(bf16[4,128,128]{2,1,0:T(8,128)(2,1)S(1)} %fusion.72), channel_id=1, source_target_pairs={{0,4},{4,8},{8,12},{12,16},{16,20},{20,24},{24,28},{1,5},{5,9},{9,... | collective-permute-start | bytes 393224 | tf_op jit(solution)/shard_map/while/body/eval_jaxpr/ppermute | solution.py:13
  308.5 6.3 %collective-permute-start = (bf16[4,128,128]{2,1,0:T(8,128)(2,1)S(1)}, bf16[4,128,128]{2,1,0:T(8,128)(2,1)S(1)}, u32[]{:S(2)}, u32[]{:S(2)}) collective-permute-start(bf16[4,128,128]{2,1,0:T(8,128)(2,1)S(1)} %fusion.72), channel_id=1, source_target_pairs={{0,4},{4,8},{8,12},{12,16},{16,20},{20,24},{24,28},{1,5},{5,9},{9,... | collective-permute-start | bytes 393224 | tf_op jit(solution)/shard_map/while/body/eval_jaxpr/ppermute | solution.py:13
  314.8 4.9 %copy-start.3 = (f32[1024,512]{0,1:T(8,128)S(1)}, f32[1024,512]{0,1:T(8,128)}, u32[]{:S(2)}) copy-start(f32[1024,512]{0,1:T(8,128)} %copy.52) | copy-start | bytes 6291460
Sparse Core Ops, SparseCore 0:
  11.5 80.2 all-gather.1
  324.7 85.5 reduce-scatter.1
where the time goes:
time: 424 us; the launch traced here: 420 us
  waiting for transfers between devices  194 us (46%)
  local copies, waits for them, and re-layouts  96.7 us (23%)
  matrix products  50.3 us (12%)
  other arithmetic  44.2 us (10%)
  between operations  15.5 us (4%)
  loops' own time  9.8 us (2%)
  starting transfers between devices  9.13 us (2%)
    reduce_scatter x1, waiting for transfers between devices, local(): lax.psum_scatter(jnp.dot(gated, w_out, preferred_element_type=jnp.float32...  84.9 us
    all_gather x1, waiting for transfers between devices, local(): piece = lax.all_gather(normed, 'head', axis=0, tiled=True)  77.5 us
    dynamic_update_slice x8, local copies, waits for them, and re-layouts, local(): lax.scan(span_pass, (start_state, prev_doc), inputs)  65.8 us
    ppermute x7, waiting for transfers between devices, passed_along(): return lax.ppermute(shard, axis, pairs)  32 us
    dot_general x5, matrix products, local(): jnp.dot(piece, matrix, preferred_element_type=jnp.float32)  24.3 us
    mul x8, other arithmetic, span_pass(): scaled_k * end_decay[None]  9.57 us
    another operation x1, loops' own time, local(): lax.scan(span_pass, (start_state, prev_doc), inputs)  9.56 us
    reshape x4, local copies, waits for them, and re-layouts, blocks(): return array.reshape(spans, SPAN, group_heads, DK)  9.42 us
  transfers between devices with their start and end apart: 9, of which 9 were waited for; matrix products, arithmetic and copies ran while one was open for 1% of the time, Pallas kernels for 0%

commit v1 on v0

v1 whole, which is shorter than its diff:
```python
import functools

import jax
import jax.numpy as jnp
from jax import lax
from jax.experimental import pallas as pl
from jax.experimental.pallas import tpu as pltpu
from jax.sharding import PartitionSpec as P

DK = 128
MESH = pl.DeviceIdType.MESH
NT = (((1,), (1,)), ((), ()))
TN = (((0,), (0,)), ((), ()))
F32, BF16 = jnp.float32, jnp.bfloat16


def dot(a, b, dims=(((1,), (0,)), ((), ()))):
    return lax.dot_general(a, b, dims, preferred_element_type=F32)


def block_by_distance(i, z, n):
    up = jnp.where(2 * z < n, 1, -1)
    near = jnp.where(2 * z < n, z, n - 1 - z)
    half = (i + 1) // 2
    paired = jnp.where(i % 2 == 1, z + up * half, z - up * half)
    single = jnp.where(2 * z < n, i, n - 1 - i)
    return jnp.where(i <= 2 * near, paired, single)


def project_kernel(
    n, tokens_ref, rate_ref, doc_col, doc_row, prev_ref, wq, wk, wv, wg, wf,
    local_ref, cq_ref, gate_ref, state_ref, decay_ref,
    gathered, weights, load_sem, send_sem, recv_sem,
):
    z = lax.axis_index("head")
    loads = [
        pltpu.make_async_copy(w, weights.at[i], load_sem.at[i])
        for i, w in enumerate((wf, wq, wk, wv, wg))
    ]
    for load in loads:
        load.start()

    barrier = pltpu.get_barrier_semaphore()

    @pl.when(z > 0)
    def _():
        pl.semaphore_signal(barrier, inc=1, device_id={"head": z - 1}, device_id_type=MESH)

    @pl.when(z < n - 1)
    def _():
        pl.semaphore_signal(barrier, inc=1, device_id={"head": z + 1}, device_id_type=MESH)

    tokens = tokens_ref[...].astype(F32)
    scale = lax.rsqrt(jnp.mean(tokens * tokens, axis=-1, keepdims=True) + 1e-05)
    gathered[z] = (tokens * scale).astype(BF16)

    peers = jnp.where(z > 0, 1, 0) + jnp.where(z < n - 1, 1, 0)
    pl.semaphore_wait(barrier, peers)

    def pass_on(b, way):
        return pltpu.make_async_remote_copy(
            src_ref=gathered.at[b],
            dst_ref=gathered.at[b],
            send_sem=send_sem.at[(way + 1) // 2, b],
            recv_sem=recv_sem.at[b],
            device_id={"head": z + way},
            device_id_type=MESH,
        )

    rows = tokens_ref.shape[0]
    half = rows // 2
    width = rate_ref.shape[1]
    row_at = lax.broadcasted_iota(jnp.int32, (rows, rows), 0)
    col_at = lax.broadcasted_iota(jnp.int32, (rows, rows), 1)
    lower = row_at >= col_at
    lower_bf = lower.astype(F32).astype(BF16)

    def step(i, carry):
        b = block_by_distance(i, z, n)

        @pl.when(i > 0)
        def _():
            pltpu.make_async_remote_copy(
                src_ref=gathered.at[b],
                dst_ref=gathered.at[b],
                send_sem=send_sem.at[0, b],
                recv_sem=recv_sem.at[b],
                device_id={"head": z},
                device_id_type=MESH,
            ).wait_recv()

        @pl.when((b <= z) & (z < n - 1))
        def _():
            pass_on(b, 1).start()

        @pl.when((b >= z) & (z > 0))
        def _():
            pass_on(b, -1).start()

        @pl.when(i == 0)
        def _():
            for load in loads:
                load.wait()

        x = gathered[b]
        logit = dot(x, weights[0])
        softplus = jnp.maximum(logit, 0.0) + jnp.log1p(jnp.exp(-jnp.abs(logit)))
        log_decay = -rate_ref[...] * softplus
        high = log_decay.astype(BF16)
        low = (log_decay - high.astype(F32)).astype(BF16)
        cum = dot(lower_bf, high) + dot(lower_bf, low)
        q = dot(x, weights[1]).astype(BF16).astype(F32)
        k = dot(x, weights[2]).astype(BF16).astype(F32)
        v = dot(x, weights[3]).astype(BF16)
        gate_ref[b] = dot(x, weights[4]).astype(BF16)

        docs = doc_col[b]
        same = lower & (docs == doc_row[b])
        last_doc = docs[rows - 1 :, :]
        prev = prev_ref[b]
        carried = (docs == prev).astype(F32)
        ending = (docs == last_doc).astype(F32)
        keep = (last_doc == prev).astype(F32)
        last = cum[rows - 1 :, :]
        middle = cum[half - 1 : half, :]
        decay_ref[b] = jnp.exp(last) * keep
        cq_ref[b] = (q * jnp.exp(cum) * carried).astype(BF16)
        k_end = (k * jnp.exp(last - cum) * ending).astype(BF16)
        top, low_half = slice(0, half), slice(half, rows)
        top_mid, low_mid = 0.5 * middle, 0.5 * (middle + last)
        q_top = (q[top] * jnp.exp(cum[top] - top_mid)).astype(BF16)
        k_top = (k[top] * jnp.exp(top_mid - cum[top])).astype(BF16)
        q_low = (q[low_half] * jnp.exp(cum[low_half] - low_mid)).astype(BF16)
        k_low = (k[low_half] * jnp.exp(low_mid - cum[low_half])).astype(BF16)
        q_cross = (q[low_half] * jnp.exp(cum[low_half] - middle)).astype(BF16)
        k_cross = (k[top] * jnp.exp(middle - cum[top])).astype(BF16)
        for h in range(width // DK):
            c = slice(h * DK, (h + 1) * DK)
            s_top = jnp.where(same[top, top], dot(q_top[:, c], k_top[:, c], NT), 0.0)
            s_cross = jnp.where(same[low_half, top], dot(q_cross[:, c], k_cross[:, c], NT), 0.0)
            s_low = jnp.where(
                same[low_half, low_half], dot(q_low[:, c], k_low[:, c], NT), 0.0
            )
            local_ref[b, top, c] = dot(s_top.astype(BF16), v[top, c])
            s_both = jnp.concatenate([s_cross, s_low], axis=1).astype(BF16)
            local_ref[b, low_half, c] = dot(s_both, v[:, c])
            state_ref[b, h] = dot(v[:, c], k_end[:, c], TN)
        return carry

    lax.fori_loop(0, n, step, 0)

    def finish(i, carry):
        @pl.when((i <= z) & (z < n - 1))
        def _():
            pass_on(i, 1).wait_send()

        @pl.when((i >= z) & (z > 0))
        def _():
            pass_on(i, -1).wait_send()

        return carry

    lax.fori_loop(0, n, finish, 0)


def output_kernel(
    n, tokens_ref, local_ref, cq_ref, gate_ref, state_ref, w_ref, out_ref,
    sending, arrived, weights, load_sem, send_sem, recv_sem,
):
    z = lax.axis_index("head")
    load = pltpu.make_async_copy(w_ref, weights, load_sem)
    load.start()
    barrier = pltpu.get_barrier_semaphore()
    for away in range(1, n):
        pl.semaphore_signal(
            barrier, inc=1, device_id={"head": (z + away) % n}, device_id_type=MESH
        )
    pl.semaphore_wait(barrier, n - 1)
    width = cq_ref.shape[2]

    def send(b):
        return pltpu.make_async_remote_copy(
            src_ref=sending.at[b],
            dst_ref=arrived.at[z],
            send_sem=send_sem.at[b],
            recv_sem=recv_sem.at[z],
            device_id={"head": b},
            device_id_type=MESH,
        )

    def gated(i, carry):
        b = block_by_distance(n - 1 - i, z, n)
        for h in range(width // DK):
            c = slice(h * DK, (h + 1) * DK)
            mixed = local_ref[b, :, c] + dot(cq_ref[b, :, c], state_ref[b, h], NT)
            inverse = lax.rsqrt(jnp.mean(mixed * mixed, axis=-1, keepdims=True) + 1e-05)
            gate = gate_ref[b, :, c].astype(F32)
            sending[b, :, c] = (mixed * inverse * (gate * jax.nn.sigmoid(gate))).astype(BF16)

        @pl.when(i < n - 1)
        def _():
            send(b).start()

        return carry

    lax.fori_loop(0, n, gated, 0)
    load.wait()
    out = tokens_ref[...].astype(F32) + dot(sending[z], weights[z])
    for away in range(1, n):
        b = block_by_distance(away, z, n)
        pltpu.make_async_remote_copy(
            src_ref=sending.at[b],
            dst_ref=arrived.at[b],
            send_sem=send_sem.at[b],
            recv_sem=recv_sem.at[b],
            device_id={"head": b},
            device_id_type=MESH,
        ).wait_recv()
        out = out + dot(arrived[b], weights[b])
    out_ref[...] = out.astype(BF16)
    for away in range(1, n):
        send((z + away) % n).wait_send()


def local(tokens, lengths, w_query, w_key, w_value, w_gate, w_forget, decay_rate, w_out):
    n, segs = lax.axis_size("head"), lax.axis_size("seq")
    seq = lax.axis_index("seq")
    rows, features = tokens.shape
    width = w_query.shape[1]
    heads = width // DK
    seg_len = rows * n

    piece_rows = width // segs
    own_piece = lax.dynamic_slice_in_dim(w_out, seq * piece_rows, piece_rows, 0)
    w_full = lax.all_gather(own_piece, ("head", "seq"), axis=0, tiled=True)
    w_full = w_full.reshape(n, width, features)

    docs_at = jnp.arange(lengths.shape[0])
    starts = jnp.sum(jnp.where(docs_at[None, :] < docs_at[:, None], lengths[None, :], 0), axis=1)
    positions = seq * seg_len - 1 + jnp.arange(seg_len + 1, dtype=jnp.int32)
    doc_ids = jnp.sum((starts[None, :] <= positions[:, None]).astype(jnp.int32), axis=1) - 1
    own_docs = doc_ids[1:].reshape(n, rows)
    prev = doc_ids[:-1].reshape(n, rows)[:, :1].reshape(n, 1, 1)

    vmem, anywhere = pl.BlockSpec(memory_space=pltpu.VMEM), pl.BlockSpec(memory_space=pl.ANY)
    shape = jax.ShapeDtypeStruct
    within, carried_q, gates, block_state, block_decay = pl.pallas_call(
        functools.partial(project_kernel, n),
        out_shape=(
            shape((n, rows, width), F32),
            shape((n, rows, width), BF16),
            shape((n, rows, width), BF16),
            shape((n, heads, DK, DK), F32),
            shape((n, 1, width), F32),
        ),
        in_specs=[vmem] * 5 + [anywhere] * 5,
        out_specs=(vmem,) * 5,
        scratch_shapes=[
            pltpu.VMEM((n, rows, features), BF16),
            pltpu.VMEM((5, features, width), BF16),
            pltpu.SemaphoreType.DMA((5,)),
            pltpu.SemaphoreType.DMA((2, n)),
            pltpu.SemaphoreType.DMA((n,)),
        ],
        compiler_params=pltpu.CompilerParams(
            collective_id=0, has_side_effects=True, vmem_limit_bytes=50 * 2**20
        ),
        cost_estimate=pl.CostEstimate(
            flops=80 * seg_len * features * width, bytes_accessed=12 * features * width, transcendentals=0
        ),
        name="project",
    )(
        tokens, decay_rate[None, :], own_docs[:, :, None], own_docs[:, None, :], prev,
        w_query, w_key, w_value, w_gate, w_forget,
    )

    block_state, block_decay, w_full = lax.optimization_barrier((block_state, block_decay, w_full))
    decays = block_decay.reshape(n, heads, 1, DK)
    seg_state, seg_decay = block_state[0], decays[0]
    for b in range(1, n):
        seg_state = seg_state * decays[b] + block_state[b]
        seg_decay = seg_decay * decays[b]
    high = seg_decay.astype(BF16)
    rest = seg_decay - high.astype(F32)
    low = rest.astype(BF16)
    packet = jnp.concatenate(
        [seg_state.astype(BF16), high, low, jnp.zeros((heads, 14, DK), BF16)], axis=1
    )
    packets = lax.all_gather(packet, "seq", axis=0, tiled=False).astype(F32)
    incoming = jnp.zeros((heads, DK, DK), F32)
    for j in range(segs - 1):
        decay_j = packets[j, :, DK : DK + 1] + packets[j, :, DK + 1 : DK + 2]
        incoming = jnp.where(j < seq, incoming * decay_j + packets[j, :, :DK], incoming)
    end_state = jnp.swapaxes(seg_decay * incoming + seg_state, 1, 2)
    entering = [incoming]
    for b in range(n - 1):
        entering.append(entering[-1] * decays[b] + block_state[b])
    entering = jnp.stack(entering).astype(BF16)

    output = pl.pallas_call(
        functools.partial(output_kernel, n),
        out_shape=shape((rows, features), BF16),
        in_specs=[vmem] * 5 + [anywhere],
        out_specs=vmem,
        scratch_shapes=[
            pltpu.VMEM((n, rows, width), BF16),
            pltpu.VMEM((n, rows, width), BF16),
            pltpu.VMEM((n, width, features), BF16),
            pltpu.SemaphoreType.DMA,
            pltpu.SemaphoreType.DMA((n,)),
            pltpu.SemaphoreType.DMA((n,)),
        ],
        compiler_params=pltpu.CompilerParams(
            collective_id=1, has_side_effects=True, vmem_limit_bytes=50 * 2**20
        ),
        cost_estimate=pl.CostEstimate(
            flops=2 * rows * n * width * features, bytes_accessed=8 * features * width, transcendentals=0
        ),
        name="mix_out",
    )(tokens, within, carried_q, gates, entering, w_full)
    return (output, end_state[None])


def solution(mesh):
    in_specs = (
        P(("seq", "head"), None),
        P(),
        P(None, "head"),
        P(None, "head"),
        P(None, "head"),
        P(None, "head"),
        P(None, "head"),
        P("head"),
        P("head", None),
    )
    out_specs = (P(("seq", "head"), None), P("seq", "head", None, None))
    return jax.shard_map(local, mesh=mesh, in_specs=in_specs, out_specs=out_specs, check_vma=False)
```

time: 424 us -> 204 us (0.48)
  waiting for transfers between devices: 194 us -> 31.6 us
  Pallas kernels: 0 us -> 139 us
  local copies, waits for them, and re-layouts: 96.7 us -> 11.3 us
  matrix products: 50.3 us -> 0 us
  other arithmetic: 44.2 us -> 5.28 us
  loops' own time: 9.8 us -> 0 us
  starting transfers between devices: 9.13 us -> 0.08 us
    pallas_call x0 -> x2, Pallas kernels: none -> 139 us  [the longest x1 109 us: local(): pl.pallas_call(functools.partial(project_kernel, n), out_shape=(shape((n,...]
    reduce_scatter x1 -> x0, waiting for transfers between devices: 84.9 us -> none  [local(): lax.psum_scatter(jnp.dot(gated, w_out, preferred_element_type=jnp.float32...]
    dynamic_update_slice x8 -> x0, local copies, waits for them, and re-layouts: 65.8 us -> none  [local(): lax.scan(span_pass, (start_state, prev_doc), inputs)]
    dot_general x39 -> x0, matrix products: 50.3 us -> none  [the longest x5 24.3 us: local(): jnp.dot(piece, matrix, preferred_element_type=jnp.float32)]
    all_gather x1 -> x2, waiting for transfers between devices: 77.5 us -> 31.6 us  [the longest x1 31.6 us: local(): packets = lax.all_gather(packet, 'seq', axis=0, tiled=False).astype(F32)]
    ppermute x7 -> x0, waiting for transfers between devices: 32 us -> none  [passed_along(): return lax.ppermute(shard, axis, pairs)]
    reshape x7 -> x1, local copies, waits for them, and re-layouts: 15.1 us -> 0.01 us  [local(): prev = doc_ids[:-1].reshape(n, rows)[:, :1].reshape(n, 1, 1)]
    mul x19 -> x1, other arithmetic: 15 us -> 0.01 us  [local(): seg_decay = seg_decay * decays[b]]
  transfers between devices with their start and end apart: 9 -> 2, of which waited for: 9 -> 1; matrix products, arithmetic and copies ran while one was open for 1% -> 1% of each run, Pallas kernels for 0% -> 54%
where the time goes in v1:
time: 204 us; the launch traced here: 202 us
  Pallas kernels  139 us (68%)
  waiting for transfers between devices  31.6 us (15%)
  between operations  14.2 us (7%)
  local copies, waits for them, and re-layouts  11.3 us (6%)
  other arithmetic  5.28 us (3%)
    pallas_call x1, Pallas kernels, local(): pl.pallas_call(functools.partial(project_kernel, n), out_shape=(shape((n,...  109 us
    all_gather x1, waiting for transfers between devices, local(): packets = lax.all_gather(packet, 'seq', axis=0, tiled=False).astype(F32)  31.6 us
    pallas_call x1, Pallas kernels, local(): pl.pallas_call(functools.partial(output_kernel, n), out_shape=shape((rows...  29.7 us
    unnamed x18, local copies, waits for them, and re-layouts  9.32 us
  transfers between devices with their start and end apart: 2, of which 1 were waited for; matrix products, arithmetic and copies ran while one was open for 1% of the time, Pallas kernels for 54%

profile of v1, /device:TPU:23, one launch (start us, length us, event | category | flops | bytes accessed | tf_op | source)
XLA Modules:
  0.0 201.7 jit_solution(2377853142571756694)
XLA Ops:
  7.2 0.0 copy-start
  7.2 0.0 all-gather.4.cloned.1.call-start
  7.2 1.5 copy-done
  8.8 0.7 constant_dynamic-slice_fusion
  9.5 0.0 all-gather.4.cloned.1.call-update
  9.5 0.0 all-gather.6.cloned.1.call-start
  9.6 0.8 select_reduce_fusion
  10.3 0.1 convert_reduce_fusion
  10.5 0.1 fusion.18
  10.5 1.1 broadcast_in_dim_reshape.8.doc_col
  11.7 0.1 pad.7.clone
  11.8 0.0 copy-start.5
  11.8 1.0 copy-done.5
  12.8 0.0 copy-start.6
  12.8 0.7 copy-done.6
  13.5 109.4 %project.1 = (f32[4,256,512]{2,1,0:T(8,128)}, bf16[4,256,512]{2,1,0:T(8,128)(2,1)S(1)}, bf16[4,256,512]{2,1,0:T(8,128)(2,1)S(1)}, f32[4,4,128,128]{3,2,1,0:T(8,128)S(1)}, f32[4,1,512]{2,1,0:T(1,128)S(1)}) custom-call(bf16[256,2048]{1,0:T(8,128)(2,1)} %tokens_ref.3, f32[1,512]{1,0:T(1,128)S(1)} %bitcast.98, s32[4,256,1]{2,1,0:T(8,128)S(1)} %copy-done.5, ...), custom_call_target="tpu_custom_call" | custom-call | flops 85899345920 | bytes 12582912 | tf_op jit(solution)/shard_map/project/pallas_call | solution.py:247
  122.9 0.0 copy-start.2
  122.9 1.0 copy-done.2
  123.9 0.0 copy-start.4
  123.9 1.0 copy-done.4
  124.8 0.0 all-gather.4.cloned.1.call-done
  124.9 0.8 fusion.17
  125.6 0.8 maximum_maximum_fusion
  126.4 0.0 all-gather.6.cloned.1.call-update
  126.5 31.6 %all-gather.6.cloned.1.call-done = bf16[32,144,128]{2,1,0:T(8,128)(2,1)} async-done(((bf16[4,144,128]{2,1,0:T(8,128)(2,1)}), bf16[32,144,128]{2,1,0:T(8,128)(2,1)}) %all-gather.6.cloned.1.call-update) | async-done | bytes 1179664 | tf_op jit(solution)/shard_map/all_gather | solution.py:289
  158.1 0.0 copy-start.7
  158.1 1.5 convert.16
  159.6 0.2 fusion.15
  159.8 0.0 copy-done.7
  159.8 0.9 fusion.3
  160.8 1.8 copy.24
  162.6 0.0 copy-start.1
  162.6 0.0 copy-start.3
  162.6 0.1 fusion.16
  162.7 0.1 pad_maximum_fusion.state_ref
  162.8 1.0 copy-done.1
  163.8 0.3 copy-done.3
  164.1 29.7 %mix_out.1 = bf16[256,2048]{1,0:T(8,128)(2,1)S(1)} custom-call(bf16[256,2048]{1,0:T(8,128)(2,1)S(1)} %copy-done.1, f32[4,256,512]{2,1,0:T(8,128)} %get-tuple-element.10.local_ref, bf16[4,256,512]{2,1,0:T(8,128)(2,1)S(1)} %copy-done.3, bf16[4,256,512]{2,1,0:T(8,128)(2,1)} %copy-done.4, bf16[4,4,128,128]{3,2,1,0:T(8,128)(2,1)S(1)} %pad_maximum_fusion.state_ref, ...), custom_call_target="tpu_custom_call" | custom-call | flops 2147483648 | bytes 8388608 | tf_op jit(solution)/shard_map/mix_out/pallas_call | solution.py:300
  193.8 1.0 copy.26
  (10 shorter events, 0.1 us)
Async XLA Ops:
  7.2 1.6 copy-start
  7.2 117.7 %all-gather.4.cloned.1.call-start = ((), (), s32[]{:S(2)}) async-start(), calls=%async_computation | async-start | bytes 8650752 | tf_op jit(solution)/shard_map/all_gather | solution.py:235
  9.5 148.6 %all-gather.6.cloned.1.call-start = ((), (), s32[]{:S(2)}) async-start(), calls=%async_computation.1 | async-start | bytes 1327104 | tf_op jit(solution)/shard_map/all_gather | solution.py:289
  11.8 1.0 copy-start.5
  12.8 0.7 copy-start.6
  122.9 1.0 copy-start.2
  123.9 1.0 copy-start.4
  158.1 1.8 copy-start.7
  162.6 1.2 copy-start.1
  162.6 1.5 copy-start.3
Sparse Core Ops, SparseCore 0:
  11.4 89.5 all-gather.3
  126.6 31.4 all-gather.5

commit v2 on v1

v2 whole, which is shorter than its diff:
```python
import functools

import jax
import jax.numpy as jnp
from jax import lax
from jax.experimental import pallas as pl
from jax.experimental.pallas import tpu as pltpu
from jax.sharding import PartitionSpec as P

DK = 128
MESH = pl.DeviceIdType.MESH
NT = (((1,), (1,)), ((), ()))
TN = (((0,), (0,)), ((), ()))
F32, BF16 = jnp.float32, jnp.bfloat16


def dot(a, b, dims=(((1,), (0,)), ((), ()))):
    return lax.dot_general(a, b, dims, preferred_element_type=F32)


def block_by_distance(i, z, n):
    up = jnp.where(2 * z < n, 1, -1)
    near = jnp.where(2 * z < n, z, n - 1 - z)
    half = (i + 1) // 2
    paired = jnp.where(i % 2 == 1, z + up * half, z - up * half)
    single = jnp.where(2 * z < n, i, n - 1 - i)
    return jnp.where(i <= 2 * near, paired, single)


def layer_kernel(
    n, segs, tokens_ref, rate_ref, doc_col, doc_row, prev_ref, piece_ref, wq, wk, wv, wg, wf,
    out_ref, end_ref,
    gathered, weights, w_all, local_ref, cq_ref, gate_ref, state_ref, decay_ref,
    packets, seg_state, incoming, entering, sending, arrived,
    load_sem, send_sem, recv_sem, wz_send, wz_recv, wp_send, wp_recv, wc_send, wc_recv,
    state_send, state_recv, mix_send, mix_recv,
):
    z, seq = lax.axis_index("head"), lax.axis_index("seq")
    chips = segs // 2
    chip, core = seq // 2, seq % 2
    rows, features = tokens_ref.shape
    half = rows // 2
    width = rate_ref.shape[1]
    heads = width // DK
    loads = [
        pltpu.make_async_copy(w, weights.at[i], load_sem.at[i])
        for i, w in enumerate((wf, wq, wk, wv, wg))
    ]
    for load in loads:
        load.start()

    barrier = pltpu.get_barrier_semaphore()

    def greet_seq(away, carry):
        pl.semaphore_signal(
            barrier, inc=1, device_id={"seq": (seq + away) % segs}, device_id_type=MESH
        )
        return carry

    def greet_head(away, carry):
        pl.semaphore_signal(
            barrier, inc=1, device_id={"head": (z + away) % n}, device_id_type=MESH
        )
        return carry

    lax.fori_loop(1, segs, greet_seq, 0)
    lax.fori_loop(1, n, greet_head, 0)

    tokens = tokens_ref[...].astype(F32)
    scale = lax.rsqrt(jnp.mean(tokens * tokens, axis=-1, keepdims=True) + 1e-05)
    gathered[z] = (tokens * scale).astype(BF16)
    w_all[z, core, chip] = piece_ref[...]
    pl.semaphore_wait(barrier, segs - 1 + n - 1)

    def pass_tokens(b, way):
        return pltpu.make_async_remote_copy(
            src_ref=gathered.at[b],
            dst_ref=gathered.at[b],
            send_sem=send_sem.at[(way + 1) // 2, b],
            recv_sem=recv_sem.at[b],
            device_id={"head": (z + way + n) % n},
            device_id_type=MESH,
        )

    def pass_piece(b, way):
        return pltpu.make_async_remote_copy(
            src_ref=w_all.at[b, core, chip],
            dst_ref=w_all.at[b, core, chip],
            send_sem=wz_send.at[(way + 1) // 2, b],
            recv_sem=wz_recv.at[b],
            device_id={"head": (z + way + n) % n},
            device_id_type=MESH,
        )

    def spread_piece(b, source, target):
        return pltpu.make_async_remote_copy(
            src_ref=w_all.at[b, core, source],
            dst_ref=w_all.at[b, core, source],
            send_sem=wp_send.at[b, target],
            recv_sem=wp_recv.at[b, source],
            device_id={"seq": 2 * target + core},
            device_id_type=MESH,
        )

    def share_pieces(b, from_core):
        return pltpu.make_async_remote_copy(
            src_ref=w_all.at[b, from_core],
            dst_ref=w_all.at[b, from_core],
            send_sem=wc_send.at[b],
            recv_sem=wc_recv.at[b],
            device_id={"seq": 2 * chip + 1 - core},
            device_id_type=MESH,
        )

    def both_ways(b, copy, act):
        @pl.when((b <= z) & (z < n - 1))
        def _():
            act(copy(b, 1))

        @pl.when((b >= z) & (z > 0))
        def _():
            act(copy(b, -1))

    def start(copy):
        copy.start()

    def wait_send(copy):
        copy.wait_send()

    def share_after_spread(b):
        def arrival(away, carry):
            spread_piece(b, (chip + away) % chips, (chip + away) % chips).wait_recv()
            return carry

        lax.fori_loop(1, chips, arrival, 0)
        share_pieces(b, core).start()

    row_at = lax.broadcasted_iota(jnp.int32, (rows, rows), 0)
    col_at = lax.broadcasted_iota(jnp.int32, (rows, rows), 1)
    lower = row_at >= col_at
    lower_bf = lower.astype(F32).astype(BF16)

    def step(i, carry):
        b = block_by_distance(i, z, n)

        @pl.when(i > 0)
        def _():
            pass_piece(b, 1).wait_recv()

        both_ways(b, pass_piece, start)

        @pl.when(i > 0)
        def _():
            pass_tokens(b, 1).wait_recv()

        both_ways(b, pass_tokens, start)

        def spread(away, inner):
            spread_piece(b, chip, (chip + away) % chips).start()
            return inner

        lax.fori_loop(1, chips, spread, 0)

        @pl.when(i > 0)
        def _():
            share_after_spread(block_by_distance(i - 1, z, n))

        @pl.when(i == 0)
        def _():
            for load in loads:
                load.wait()

        x = gathered[b]
        logit = dot(x, weights[0])
        softplus = jnp.maximum(logit, 0.0) + jnp.log1p(jnp.exp(-jnp.abs(logit)))
        log_decay = -rate_ref[...] * softplus
        high = log_decay.astype(BF16)
        low = (log_decay - high.astype(F32)).astype(BF16)
        cum = dot(lower_bf, high) + dot(lower_bf, low)
        q = dot(x, weights[1]).astype(BF16).astype(F32)
        k = dot(x, weights[2]).astype(BF16).astype(F32)
        v = dot(x, weights[3]).astype(BF16)
        gate_ref[b] = dot(x, weights[4]).astype(BF16)

        docs = doc_col[b]
        same = lower & (docs == doc_row[b])
        last_doc = docs[rows - 1 :, :]
        prev = prev_ref[b]
        carried = (docs == prev).astype(F32)
        ending = (docs == last_doc).astype(F32)
        keep = (last_doc == prev).astype(F32)
        last = cum[rows - 1 :, :]
        middle = cum[half - 1 : half, :]
        decay_ref[b] = jnp.exp(last) * keep
        cq_ref[b] = (q * jnp.exp(cum) * carried).astype(BF16)
        k_end = (k * jnp.exp(last - cum) * ending).astype(BF16)
        top, low_half = slice(0, half), slice(half, rows)
        top_mid, low_mid = 0.5 * middle, 0.5 * (middle + last)
        q_top = (q[top] * jnp.exp(cum[top] - top_mid)).astype(BF16)
        k_top = (k[top] * jnp.exp(top_mid - cum[top])).astype(BF16)
        q_low = (q[low_half] * jnp.exp(cum[low_half] - low_mid)).astype(BF16)
        k_low = (k[low_half] * jnp.exp(low_mid - cum[low_half])).astype(BF16)
        q_cross = (q[low_half] * jnp.exp(cum[low_half] - middle)).astype(BF16)
        k_cross = (k[top] * jnp.exp(middle - cum[top])).astype(BF16)
        for h in range(width // DK):
            c = slice(h * DK, (h + 1) * DK)
            s_top = jnp.where(same[top, top], dot(q_top[:, c], k_top[:, c], NT), 0.0)
            s_cross = jnp.where(same[low_half, top], dot(q_cross[:, c], k_cross[:, c], NT), 0.0)
            s_low = jnp.where(
                same[low_half, low_half], dot(q_low[:, c], k_low[:, c], NT), 0.0
            )
            local_ref[b, top, c] = dot(s_top.astype(BF16), v[top, c])
            s_both = jnp.concatenate([s_cross, s_low], axis=1).astype(BF16)
            local_ref[b, low_half, c] = dot(s_both, v[:, c])
            state_ref[b, h] = dot(v[:, c], k_end[:, c], TN)
        return carry

    lax.fori_loop(0, n, step, 0)

    def send_state(to):
        return pltpu.make_async_remote_copy(
            src_ref=packets.at[seq],
            dst_ref=packets.at[seq],
            send_sem=state_send.at[to],
            recv_sem=state_recv.at[seq],
            device_id={"seq": to},
            device_id_type=MESH,
        )

    seg_decay = decay_ref[0]
    for b in range(1, n):
        seg_decay = seg_decay * decay_ref[b]
    high = seg_decay.astype(BF16).astype(F32)
    low = seg_decay - high
    pad_at = lax.broadcasted_iota(jnp.int32, (16, DK), 0)
    for h in range(heads):
        c = slice(h * DK, (h + 1) * DK)
        total = state_ref[0, h]
        for b in range(1, n):
            total = total * decay_ref[b][:, c] + state_ref[b, h]
        seg_state[h] = total
        packets[seq, h, :DK] = total.astype(BF16)
        pad = jnp.where(pad_at == 0, high[:, c], jnp.where(pad_at == 1, low[:, c], 0.0))
        packets[seq, h, DK:] = pad.astype(BF16)

    def send_later(away, carry):
        @pl.when(seq + away < segs)
        def _():
            send_state(seq + away).start()

        return carry

    lax.fori_loop(1, segs, send_later, 0)
    share_after_spread(block_by_distance(n - 1, z, n))

    incoming[...] = jnp.zeros_like(incoming)

    def take(j, carry):
        @pl.when(j < seq)
        def _():
            pltpu.make_async_remote_copy(
                src_ref=packets.at[j],
                dst_ref=packets.at[j],
                send_sem=state_send.at[j],
                recv_sem=state_recv.at[j],
                device_id={"seq": (seq + 1) % segs},
                device_id_type=MESH,
            ).wait_recv()
            for h in range(heads):
                pad = packets[j, h, DK:].astype(F32)
                decay = pad[0:1] + pad[1:2]
                incoming[h] = incoming[h] * decay + packets[j, h, :DK].astype(F32)

        return carry

    lax.fori_loop(0, segs - 1, take, 0)
    for h in range(heads):
        c = slice(h * DK, (h + 1) * DK)
        held = incoming[h]
        end_ref[h] = (held * seg_decay[:, c] + seg_state[h]).T
        for b in range(n):
            entering[b, h] = held.astype(BF16)
            if b < n - 1:
                held = held * decay_ref[b][:, c] + state_ref[b, h]

    def send_mix(b):
        return pltpu.make_async_remote_copy(
            src_ref=sending.at[b],
            dst_ref=arrived.at[z],
            send_sem=mix_send.at[b],
            recv_sem=mix_recv.at[z],
            device_id={"head": b},
            device_id_type=MESH,
        )

    def gated(i, carry):
        b = block_by_distance(n - 1 - i, z, n)
        for h in range(heads):
            c = slice(h * DK, (h + 1) * DK)
            mixed = local_ref[b, :, c] + dot(cq_ref[b, :, c], entering[b, h], NT)
            inverse = lax.rsqrt(jnp.mean(mixed * mixed, axis=-1, keepdims=True) + 1e-05)
            gate = gate_ref[b, :, c].astype(F32)
            sending[b, :, c] = (mixed * inverse * (gate * jax.nn.sigmoid(gate))).astype(BF16)

        @pl.when(i < n - 1)
        def _():
            send_mix(b).start()

        return carry

    lax.fori_loop(0, n, gated, 0)

    def whole(b):
        share_pieces(b, 1 - core).wait_recv()
        return w_all[b].reshape(width, features)

    out = tokens_ref[...].astype(F32) + dot(sending[z], whole(z))
    for away in range(1, n):
        b = block_by_distance(away, z, n)
        w_b = whole(b)
        pltpu.make_async_remote_copy(
            src_ref=sending.at[b],
            dst_ref=arrived.at[b],
            send_sem=mix_send.at[b],
            recv_sem=mix_recv.at[b],
            device_id={"head": b},
            device_id_type=MESH,
        ).wait_recv()
        out = out + dot(arrived[b], w_b)
    out_ref[...] = out.astype(BF16)

    def finish(b, carry):
        both_ways(b, pass_tokens, wait_send)
        both_ways(b, pass_piece, wait_send)
        share_pieces(b, core).wait_send()

        def spread_done(away, inner):
            spread_piece(b, chip, (chip + away) % chips).wait_send()
            return inner

        lax.fori_loop(1, chips, spread_done, 0)

        @pl.when(b != z)
        def _():
            send_mix(b).wait_send()

        return carry

    lax.fori_loop(0, n, finish, 0)

    def later_done(away, carry):
        @pl.when(seq + away < segs)
        def _():
            send_state(seq + away).wait_send()

        return carry

    lax.fori_loop(1, segs, later_done, 0)


def local(tokens, lengths, w_query, w_key, w_value, w_gate, w_forget, decay_rate, w_out):
    n, segs = lax.axis_size("head"), lax.axis_size("seq")
    seq = lax.axis_index("seq")
    rows, features = tokens.shape
    width = w_query.shape[1]
    heads = width // DK
    seg_len = rows * n
    chips = segs // 2

    piece_rows = width // segs
    piece_at = ((seq % 2) * chips + seq // 2) * piece_rows
    own_piece = lax.dynamic_slice_in_dim(w_out, piece_at, piece_rows, 0)

    docs_at = jnp.arange(lengths.shape[0])
    starts = jnp.sum(jnp.where(docs_at[None, :] < docs_at[:, None], lengths[None, :], 0), axis=1)
    positions = seq * seg_len - 1 + jnp.arange(seg_len + 1, dtype=jnp.int32)
    doc_ids = jnp.sum((starts[None, :] <= positions[:, None]).astype(jnp.int32), axis=1) - 1
    own_docs = doc_ids[1:].reshape(n, rows)
    prev = doc_ids[:-1].reshape(n, rows)[:, :1].reshape(n, 1, 1)

    vmem, anywhere = pl.BlockSpec(memory_space=pltpu.VMEM), pl.BlockSpec(memory_space=pl.ANY)
    shape = jax.ShapeDtypeStruct
    dma = pltpu.SemaphoreType.DMA
    output, end_state = pl.pallas_call(
        functools.partial(layer_kernel, n, segs),
        out_shape=(shape((rows, features), BF16), shape((heads, DK, DK), F32)),
        in_specs=[vmem] * 6 + [anywhere] * 5,
        out_specs=(vmem, vmem),
        scratch_shapes=[
            pltpu.VMEM((n, rows, features), BF16),
            pltpu.VMEM((5, features, width), BF16),
            pltpu.VMEM((n, 2, chips, piece_rows, features), BF16),
            pltpu.VMEM((n, rows, width), F32),
            pltpu.VMEM((n, rows, width), BF16),
            pltpu.VMEM((n, rows, width), BF16),
            pltpu.VMEM((n, heads, DK, DK), F32),
            pltpu.VMEM((n, 1, width), F32),
            pltpu.VMEM((segs, heads, DK + 16, DK), BF16),
            pltpu.VMEM((heads, DK, DK), F32),
            pltpu.VMEM((heads, DK, DK), F32),
            pltpu.VMEM((n, heads, DK, DK), BF16),
            pltpu.VMEM((n, rows, width), BF16),
            pltpu.VMEM((n, rows, width), BF16),
            dma((5,)), dma((2, n)), dma((n,)), dma((2, n)), dma((n,)),
            dma((n, chips)), dma((n, chips)), dma((n,)), dma((n,)),
            dma((segs,)), dma((segs,)), dma((n,)), dma((n,)),
        ],
        compiler_params=pltpu.CompilerParams(
            collective_id=0, has_side_effects=True, vmem_limit_bytes=56 * 2**20
        ),
        cost_estimate=pl.CostEstimate(
            flops=12 * seg_len * features * width, bytes_accessed=14 * features * width, transcendentals=0
        ),
        name="layer",
    )(
        tokens, decay_rate[None, :], own_docs[:, :, None], own_docs[:, None, :], prev, own_piece,
        w_query, w_key, w_value, w_gate, w_forget,
    )
    return (output, end_state[None])


def solution(mesh):
    in_specs = (
        P(("seq", "head"), None),
        P(),
        P(None, "head"),
        P(None, "head"),
        P(None, "head"),
        P(None, "head"),
        P(None, "head"),
        P("head"),
        P("head", None),
    )
    out_specs = (P(("seq", "head"), None), P("seq", "head", None, None))
    return jax.shard_map(local, mesh=mesh, in_specs=in_specs, out_specs=out_specs, check_vma=False)
```

time: 204 us -> 150 us (0.74); the launches traced: 202 us -> 150 us
  waiting for transfers between devices: 31.6 us -> 0 us
  between operations: 14.2 us -> 0.7 us
  local copies, waits for them, and re-layouts: 11.3 us -> 5.58 us
  other arithmetic: 5.28 us -> 1.01 us
  Pallas kernels: 139 us -> 143 us
    all_gather x2 -> x0, waiting for transfers between devices: 31.6 us -> none  [the longest x1 31.6 us: local(): packets = lax.all_gather(packet, 'seq', axis=0, tiled=False).astype(F32)]
    unnamed x18 -> x8, local copies, waits for them, and re-layouts: 9.32 us -> 3.07 us
    pallas_call x2 -> x1, Pallas kernels: 139 us -> 143 us  [local(): pl.pallas_call(functools.partial(layer_kernel, n, segs), out_shape=(shape...]
    convert_element_type x4 -> x0, other arithmetic: 2.29 us -> none  [the longest x1 1.5 us: local(): packets = lax.all_gather(packet, 'seq', axis=0, tiled=False).astype(F32)]
  transfers between devices with their start and end apart: 2 -> 0, of which waited for: 1 -> 0; matrix products, arithmetic and copies ran while one was open for 1% -> 0% of each run, Pallas kernels for 54% -> 0%
where the time goes in v2:
time: 150 us
  Pallas kernels  143 us (95%)
  local copies, waits for them, and re-layouts  5.58 us (4%)
    pallas_call x1, Pallas kernels, local(): pl.pallas_call(functools.partial(layer_kernel, n, segs), out_shape=(shape...  143 us
    unnamed x8, local copies, waits for them, and re-layouts  3.07 us

profile of v2, /device:TPU:23, one launch (start us, length us, event | category | flops | bytes accessed | tf_op | source)
XLA Modules:
  0.0 150.1 jit_solution(18096065259120205697)
XLA Ops:
  0.6 0.0 copy-start
  0.7 0.9 select_reduce_fusion
  1.6 0.1 convert_reduce_fusion
  1.7 0.1 fusion
  1.8 0.0 copy-start.2
  1.8 0.6 slice.14
  2.4 0.0 copy-done
  2.4 0.7 constant_dynamic-slice_fusion.piece_ref
  3.1 1.1 broadcast_in_dim_reshape.8.doc_col
  4.2 0.0 copy-done.2
  4.2 142.8 %layer.1 = (bf16[256,2048]{1,0:T(8,128)(2,1)}, f32[4,128,128]{2,1,0:T(8,128)}) custom-call(bf16[256,2048]{1,0:T(8,128)(2,1)} %tokens_ref.1, f32[1,512]{1,0:T(1,128)} %bitcast.7, s32[4,256,1]{2,1,0:T(8,128)} %broadcast_in_dim_reshape.8.doc_col, s32[4,1,256]{2,1,0:T(1,128)} %bitcast.5, s32[4,1,1]{2,1,0:T(1,128)} %bitcast.6, ...), custom_call_target="tpu_custom_call" | custom-call | flops 12884901888 | bytes 14680064 | tf_op jit(solution)/shard_map/layer/pallas_call | solution.py:384
  147.0 0.0 copy-start.1
  147.0 2.3 %copy.20 = bf16[256,2048]{1,0:T(8,128)(2,1)} copy(bf16[256,2048]{1,0:T(8,128)(2,1)} %get-tuple-element.10) | data formatting | bytes 2097152
  149.4 0.0 copy-done.1
  149.4 0.7 copy.21
  (3 shorter events, 0.0 us)
Async XLA Ops:
  0.6 1.7 %copy-start = (bf16[512,2048]{1,0:T(8,128)(2,1)S(1)}, bf16[512,2048]{1,0:T(8,128)(2,1)}, u32[]{:S(2)}) copy-start(bf16[512,2048]{1,0:T(8,128)(2,1)} %param.17) | copy-start | bytes 6291460
  1.8 2.5 %copy-start.2 = (s32[1024]{0:T(1024)}, s32[1024]{0:T(1024)S(1)}, u32[]{:S(2)}) copy-start(s32[1024]{0:T(1024)S(1)} %get-tuple-element.7) | copy-start | bytes 12292
  147.0 2.4 %copy-start.1 = (f32[4,128,128]{2,1,0:T(8,128)S(1)}, f32[4,128,128]{2,1,0:T(8,128)}, u32[]{:S(2)}) copy-start(f32[4,128,128]{2,1,0:T(8,128)} %get-tuple-element.5) | copy-start | bytes 786436

commit v3 on v2

--- a/solution.py
+++ b/solution.py
@@ -8,6 +8,7 @@
 from jax.sharding import PartitionSpec as P
 
 DK = 128
+PARTS = 2
 MESH = pl.DeviceIdType.MESH
 NT = (((1,), (1,)), ((), ()))
 TN = (((0,), (0,)), ((), ()))
@@ -28,11 +29,11 @@
 
 
 def layer_kernel(
-    n, segs, tokens_ref, rate_ref, doc_col, doc_row, prev_ref, piece_ref, wq, wk, wv, wg, wf,
+    n, segs, lengths_ref, tokens_ref, rate_ref, w_out, wq, wk, wv, wg, wf,
     out_ref, end_ref,
     gathered, weights, w_all, local_ref, cq_ref, gate_ref, state_ref, decay_ref,
     packets, seg_state, incoming, entering, sending, arrived,
-    load_sem, send_sem, recv_sem, wz_send, wz_recv, wp_send, wp_recv, wc_send, wc_recv,
+    load_sem, piece_sem, send_sem, recv_sem, wz_send, wz_recv, wp_send, wp_recv, wc_send, wc_recv,
     state_send, state_recv, mix_send, mix_recv,
 ):
     z, seq = lax.axis_index("head"), lax.axis_index("seq")
@@ -48,6 +49,12 @@
     ]
     for load in loads:
         load.start()
+    piece_rows = w_all.shape[3]
+    piece_at = pl.multiple_of((core * chips + chip) * piece_rows, piece_rows)
+    own_piece = pltpu.make_async_copy(
+        w_out.at[pl.ds(piece_at, piece_rows), :], w_all.at[z, core, chip], piece_sem
+    )
+    own_piece.start()
 
     barrier = pltpu.get_barrier_semaphore()
 
@@ -69,7 +76,6 @@
     tokens = tokens_ref[...].astype(F32)
     scale = lax.rsqrt(jnp.mean(tokens * tokens, axis=-1, keepdims=True) + 1e-05)
     gathered[z] = (tokens * scale).astype(BF16)
-    w_all[z, core, chip] = piece_ref[...]
     pl.semaphore_wait(barrier, segs - 1 + n - 1)
 
     def pass_tokens(b, way):
@@ -140,30 +146,77 @@
     lower = row_at >= col_at
     lower_bf = lower.astype(F32).astype(BF16)
 
+    def doc_of(position):
+        doc = jnp.zeros(position.shape, jnp.int32)
+        begin = jnp.int32(0)
+        for j in range(lengths_ref.shape[0] - 1):
+            begin = begin + lengths_ref[j]
+            doc = doc + jnp.where(position >= begin, 1, 0)
+        return doc
+
+    up = jnp.where(2 * z < n, 1, -1)
+    near = jnp.where(2 * z < n, z, n - 1 - z)
+    far = n - 1 - near
+
+    def spread(b):
+        def one(away, carry):
+            spread_piece(b, chip, (chip + away) % chips).start()
+            return carry
+
+        lax.fori_loop(1, chips, one, 0)
+
+    def pieces_up():
+        own_piece.wait()
+        spread(z)
+
+        def tokens_left(d, carry):
+            pass_tokens(z - up * d, up).wait_send()
+            return carry
+
+        lax.fori_loop(0, near + 1, tokens_left, 0)
+        pass_piece(z, up).start()
+
+        def onward(d, carry):
+            b = z - up * d
+            pass_piece(b, up).wait_recv()
+            pass_piece(b, up).start()
+            spread(b)
+            return carry
+
+        lax.fori_loop(1, near + 1, onward, 0)
+
+    def pieces_down():
+        @pl.when(near > 0)
+        def _():
+            def tokens_left(d, carry):
+                pass_tokens(z + up * d, -up).wait_send()
+                return carry
+
+            lax.fori_loop(0, far + 1, tokens_left, 0)
+            pass_piece(z, -up).start()
+
+    def piece_down(d):
+        b = z + up * d
+        pass_piece(b, -up).wait_recv()
+
+        @pl.when(near > 0)
+        def _():
+            pass_piece(b, -up).start()
+
+        spread(b)
+
     def step(i, carry):
         b = block_by_distance(i, z, n)
 
         @pl.when(i > 0)
         def _():
-            pass_piece(b, 1).wait_recv()
-
-        both_ways(b, pass_piece, start)
-
-        @pl.when(i > 0)
-        def _():
             pass_tokens(b, 1).wait_recv()
 
         both_ways(b, pass_tokens, start)
 
-        def spread(away, inner):
-            spread_piece(b, chip, (chip + away) % chips).start()
-            return inner
-
-        lax.fori_loop(1, chips, spread, 0)
-
-        @pl.when(i > 0)
-        def _():
-            share_after_spread(block_by_distance(i - 1, z, n))
+        @pl.when(i == jnp.where(near > 0, n - 1, 1))
+        def _():
+            pieces_up()
 
         @pl.when(i == 0)
         def _():
@@ -182,10 +235,12 @@
         v = dot(x, weights[3]).astype(BF16)
         gate_ref[b] = dot(x, weights[4]).astype(BF16)
 
-        docs = doc_col[b]
-        same = lower & (docs == doc_row[b])
+        begin = seq * (rows * n) + b * rows
+        docs = doc_of(begin + lax.broadcasted_iota(jnp.int32, (rows, 1), 0))
+        docs_across = doc_of(begin + lax.broadcasted_iota(jnp.int32, (1, rows), 1))
+        same = lower & (docs == docs_across)
         last_doc = docs[rows - 1 :, :]
-        prev = prev_ref[b]
+        prev = doc_of(begin - 1 + lax.broadcasted_iota(jnp.int32, (1, 1), 0))
         carried = (docs == prev).astype(F32)
         ending = (docs == last_doc).astype(F32)
         keep = (last_doc == prev).astype(F32)
@@ -217,12 +272,14 @@
 
     lax.fori_loop(0, n, step, 0)
 
-    def send_state(to):
+    per = heads // PARTS
+
+    def send_state(part, to):
         return pltpu.make_async_remote_copy(
-            src_ref=packets.at[seq],
-            dst_ref=packets.at[seq],
-            send_sem=state_send.at[to],
-            recv_sem=state_recv.at[seq],
+            src_ref=packets.at[part, seq],
+            dst_ref=packets.at[part, seq],
+            send_sem=state_send.at[part, to],
+            recv_sem=state_recv.at[part, seq],
             device_id={"seq": to},
             device_id_type=MESH,
         )
@@ -233,104 +290,130 @@
     high = seg_decay.astype(BF16).astype(F32)
     low = seg_decay - high
     pad_at = lax.broadcasted_iota(jnp.int32, (16, DK), 0)
-    for h in range(heads):
-        c = slice(h * DK, (h + 1) * DK)
-        total = state_ref[0, h]
-        for b in range(1, n):
-            total = total * decay_ref[b][:, c] + state_ref[b, h]
-        seg_state[h] = total
-        packets[seq, h, :DK] = total.astype(BF16)
-        pad = jnp.where(pad_at == 0, high[:, c], jnp.where(pad_at == 1, low[:, c], 0.0))
-        packets[seq, h, DK:] = pad.astype(BF16)
-
-    def send_later(away, carry):
-        @pl.when(seq + away < segs)
-        def _():
-            send_state(seq + away).start()
-
-        return carry
-
-    lax.fori_loop(1, segs, send_later, 0)
-    share_after_spread(block_by_distance(n - 1, z, n))
-
+    for part in range(PARTS):
+        for i in range(per):
+            h = part * per + i
+            c = slice(h * DK, (h + 1) * DK)
+            total = state_ref[0, h]
+            for b in range(1, n):
+                total = total * decay_ref[b][:, c] + state_ref[b, h]
+            seg_state[h] = total
+            packets[part, seq, i, :DK] = total.astype(BF16)
+            pad = jnp.where(pad_at == 0, high[:, c], jnp.where(pad_at == 1, low[:, c], 0.0))
+            packets[part, seq, i, DK:] = pad.astype(BF16)
+
+        def send_later(away, carry):
+            @pl.when(seq + away < segs)
+            def _():
+                send_state(part, seq + away).start()
+
+            return carry
+
+        lax.fori_loop(1, segs, send_later, 0)
+
+    pieces_down()
+
+    def early_piece(d, carry):
+        piece_down(d)
+        return carry
+
+    lax.fori_loop(1, far, early_piece, 0)
     incoming[...] = jnp.zeros_like(incoming)
 
-    def take(j, carry):
-        @pl.when(j < seq)
-        def _():
-            pltpu.make_async_remote_copy(
-                src_ref=packets.at[j],
-                dst_ref=packets.at[j],
-                send_sem=state_send.at[j],
-                recv_sem=state_recv.at[j],
-                device_id={"seq": (seq + 1) % segs},
-                device_id_type=MESH,
-            ).wait_recv()
-            for h in range(heads):
-                pad = packets[j, h, DK:].astype(F32)
-                decay = pad[0:1] + pad[1:2]
-                incoming[h] = incoming[h] * decay + packets[j, h, :DK].astype(F32)
-
-        return carry
-
-    lax.fori_loop(0, segs - 1, take, 0)
-    for h in range(heads):
-        c = slice(h * DK, (h + 1) * DK)
-        held = incoming[h]
-        end_ref[h] = (held * seg_decay[:, c] + seg_state[h]).T
-        for b in range(n):
-            entering[b, h] = held.astype(BF16)
-            if b < n - 1:
-                held = held * decay_ref[b][:, c] + state_ref[b, h]
-
-    def send_mix(b):
+    def send_mix(part, b):
         return pltpu.make_async_remote_copy(
-            src_ref=sending.at[b],
-            dst_ref=arrived.at[z],
-            send_sem=mix_send.at[b],
-            recv_sem=mix_recv.at[z],
+            src_ref=sending.at[part, b],
+            dst_ref=arrived.at[part, z],
+            send_sem=mix_send.at[part, b],
+            recv_sem=mix_recv.at[part, z],
             device_id={"head": b},
             device_id_type=MESH,
         )
 
-    def gated(i, carry):
-        b = block_by_distance(n - 1 - i, z, n)
-        for h in range(heads):
+    for part in range(PARTS):
+
+        def take(j, carry):
+            @pl.when(j < seq)
+            def _():
+                pltpu.make_async_remote_copy(
+                    src_ref=packets.at[part, j],
+                    dst_ref=packets.at[part, j],
+                    send_sem=state_send.at[part, j],
+                    recv_sem=state_recv.at[part, j],
+                    device_id={"seq": (seq + 1) % segs},
+                    device_id_type=MESH,
+                ).wait_recv()
+                for i in range(per):
+                    h = part * per + i
+                    pad = packets[part, j, i, DK:].astype(F32)
+                    decay = pad[0:1] + pad[1:2]
+                    incoming[h] = incoming[h] * decay + packets[part, j, i, :DK].astype(F32)
+
+            return carry
+
+        lax.fori_loop(0, segs - 1, take, 0)
+        for i in range(per):
+            h = part * per + i
             c = slice(h * DK, (h + 1) * DK)
-            mixed = local_ref[b, :, c] + dot(cq_ref[b, :, c], entering[b, h], NT)
-            inverse = lax.rsqrt(jnp.mean(mixed * mixed, axis=-1, keepdims=True) + 1e-05)
-            gate = gate_ref[b, :, c].astype(F32)
-            sending[b, :, c] = (mixed * inverse * (gate * jax.nn.sigmoid(gate))).astype(BF16)
-
-        @pl.when(i < n - 1)
-        def _():
-            send_mix(b).start()
-
-        return carry
-
-    lax.fori_loop(0, n, gated, 0)
+            held = incoming[h]
+            end_ref[h] = (held * seg_decay[:, c] + seg_state[h]).T
+            for b in range(n):
+                entering[b, h] = held.astype(BF16)
+                if b < n - 1:
+                    held = held * decay_ref[b][:, c] + state_ref[b, h]
+
+        def gated(i, carry):
+            b = block_by_distance(n - 1 - i, z, n)
+            for k in range(per):
+                h = part * per + k
+                c = slice(h * DK, (h + 1) * DK)
+                mixed = local_ref[b, :, c] + dot(cq_ref[b, :, c], entering[b, h], NT)
+                inverse = lax.rsqrt(jnp.mean(mixed * mixed, axis=-1, keepdims=True) + 1e-05)
+                gate = gate_ref[b, :, c].astype(F32)
+                result = mixed * inverse * (gate * jax.nn.sigmoid(gate))
+                sending[part, b, :, k * DK : (k + 1) * DK] = result.astype(BF16)
+
+            @pl.when(i < n - 1)
+            def _():
+                send_mix(part, b).start()
+
+            return carry
+
+        lax.fori_loop(0, n, gated, 0)
+        if part == 0:
+            piece_down(far)
+
+    def share(i, carry):
+        share_after_spread(block_by_distance(i, z, n))
+        return carry
+
+    lax.fori_loop(0, n, share, 0)
+    wide = width // PARTS
 
     def whole(b):
         share_pieces(b, 1 - core).wait_recv()
         return w_all[b].reshape(width, features)
 
-    out = tokens_ref[...].astype(F32) + dot(sending[z], whole(z))
+    out = tokens_ref[...].astype(F32)
+    w_own = whole(z)
+    for part in range(PARTS):
+        out = out + dot(sending[part, z], w_own[part * wide : (part + 1) * wide])
     for away in range(1, n):
         b = block_by_distance(away, z, n)
         w_b = whole(b)
-        pltpu.make_async_remote_copy(
-            src_ref=sending.at[b],
-            dst_ref=arrived.at[b],
-            send_sem=mix_send.at[b],
-            recv_sem=mix_recv.at[b],
-            device_id={"head": b},
-            device_id_type=MESH,
-        ).wait_recv()
-        out = out + dot(arrived[b], w_b)
+        for part in range(PARTS):
+            pltpu.make_async_remote_copy(
+                src_ref=sending.at[part, b],
+                dst_ref=arrived.at[part, b],
+                send_sem=mix_send.at[part, b],
+                recv_sem=mix_recv.at[part, b],
+                device_id={"head": b},
+                device_id_type=MESH,
+            ).wait_recv()
+            out = out + dot(arrived[part, b], w_b[part * wide : (part + 1) * wide])
     out_ref[...] = out.astype(BF16)
 
     def finish(b, carry):
-        both_ways(b, pass_tokens, wait_send)
         both_ways(b, pass_piece, wait_send)
         share_pieces(b, core).wait_send()
 
@@ -342,7 +425,8 @@
 
         @pl.when(b != z)
         def _():
-            send_mix(b).wait_send()
+            for part in range(PARTS):
+                send_mix(part, b).wait_send()
 
         return carry
 
@@ -351,7 +435,8 @@
     def later_done(away, carry):
         @pl.when(seq + away < segs)
         def _():
-            send_state(seq + away).wait_send()
+            for part in range(PARTS):
+                send_state(part, seq + away).wait_send()
 
         return carry
 
@@ -360,7 +445,6 @@
 
 def local(tokens, lengths, w_query, w_key, w_value, w_gate, w_forget, decay_rate, w_out):
     n, segs = lax.axis_size("head"), lax.axis_size("seq")
-    seq = lax.axis_index("seq")
     rows, features = tokens.shape
     width = w_query.shape[1]
     heads = width // DK
@@ -368,15 +452,6 @@
     chips = segs // 2
 
     piece_rows = width // segs
-    piece_at = ((seq % 2) * chips + seq // 2) * piece_rows
-    own_piece = lax.dynamic_slice_in_dim(w_out, piece_at, piece_rows, 0)
-
-    docs_at = jnp.arange(lengths.shape[0])
-    starts = jnp.sum(jnp.where(docs_at[None, :] < docs_at[:, None], lengths[None, :], 0), axis=1)
-    positions = seq * seg_len - 1 + jnp.arange(seg_len + 1, dtype=jnp.int32)
-    doc_ids = jnp.sum((starts[None, :] <= positions[:, None]).astype(jnp.int32), axis=1) - 1
-    own_docs = doc_ids[1:].reshape(n, rows)
-    prev = doc_ids[:-1].reshape(n, rows)[:, :1].reshape(n, 1, 1)
 
     vmem, anywhere = pl.BlockSpec(memory_space=pltpu.VMEM), pl.BlockSpec(memory_space=pl.ANY)
     shape = jax.ShapeDtypeStruct
@@ -384,7 +459,7 @@
     output, end_state = pl.pallas_call(
         functools.partial(layer_kernel, n, segs),
         out_shape=(shape((rows, features), BF16), shape((heads, DK, DK), F32)),
-        in_specs=[vmem] * 6 + [anywhere] * 5,
+        in_specs=[pl.BlockSpec(memory_space=pltpu.SMEM)] + [vmem] * 2 + [anywhere] * 6,
         out_specs=(vmem, vmem),
         scratch_shapes=[
             pltpu.VMEM((n, rows, features), BF16),
@@ -395,15 +470,15 @@
             pltpu.VMEM((n, rows, width), BF16),
             pltpu.VMEM((n, heads, DK, DK), F32),
             pltpu.VMEM((n, 1, width), F32),
-            pltpu.VMEM((segs, heads, DK + 16, DK), BF16),
+            pltpu.VMEM((PARTS, segs, heads // PARTS, DK + 16, DK), BF16),
             pltpu.VMEM((heads, DK, DK), F32),
             pltpu.VMEM((heads, DK, DK), F32),
             pltpu.VMEM((n, heads, DK, DK), BF16),
-            pltpu.VMEM((n, rows, width), BF16),
-            pltpu.VMEM((n, rows, width), BF16),
-            dma((5,)), dma((2, n)), dma((n,)), dma((2, n)), dma((n,)),
+            pltpu.VMEM((PARTS, n, rows, width // PARTS), BF16),
+            pltpu.VMEM((PARTS, n, rows, width // PARTS), BF16),
+            dma((5,)), dma, dma((2, n)), dma((n,)), dma((2, n)), dma((n,)),
             dma((n, chips)), dma((n, chips)), dma((n,)), dma((n,)),
-            dma((segs,)), dma((segs,)), dma((n,)), dma((n,)),
+            dma((PARTS, segs)), dma((PARTS, segs)), dma((PARTS, n)), dma((PARTS, n)),
         ],
         compiler_params=pltpu.CompilerParams(
             collective_id=0, has_side_effects=True, vmem_limit_bytes=56 * 2**20
@@ -413,7 +488,7 @@
         ),
         name="layer",
     )(
-        tokens, decay_rate[None, :], own_docs[:, :, None], own_docs[:, None, :], prev, own_piece,
+        lengths, tokens, decay_rate[None, :], w_out,
         w_query, w_key, w_value, w_gate, w_forget,
     )
     return (output, end_state[None])

time: 150 us -> 140 us (0.933)
  the two profiles are of different devices: /device:TPU:23 before, /device:TPU:7 now
where the time goes in v3:
time: 140 us
  Pallas kernels  136 us (97%)
  local copies, waits for them, and re-layouts  3.05 us (2%)
    pallas_call x1, Pallas kernels, local(): pl.pallas_call(functools.partial(layer_kernel, n, segs), out_shape=(shape...  136 us
    unnamed x4, local copies, waits for them, and re-layouts  3.05 us

profile of v3, /device:TPU:7, one launch (start us, length us, event | category | flops | bytes accessed | tf_op | source)
XLA Modules:
  0.0 140.0 jit_solution(4402337146675950855)
XLA Ops:
  0.6 136.3 %layer.1 = (bf16[256,2048]{1,0:T(8,128)(2,1)}, f32[4,128,128]{2,1,0:T(8,128)}) custom-call(s32[16]{0:T(128)} %lengths_ref.1, bf16[256,2048]{1,0:T(8,128)(2,1)} %tokens_ref.1, f32[1,512]{1,0:T(1,128)} %bitcast.3, bf16[512,2048]{1,0:T(8,128)(2,1)} %w_out.1, bf16[2048,512]{1,0:T(8,128)(2,1)} %wq.1, bf16[2048,512]{1,0:T(8,128)(2,1)} %wk.1, ...), custom_call_target="tpu_custom_call" | custom-call | flops 12884901888 | bytes 14680064 | tf_op jit(solution)/shard_map/layer/pallas_call | solution.py:459
  136.9 0.0 copy-start
  136.9 2.3 %copy.13 = bf16[256,2048]{1,0:T(8,128)(2,1)} copy(bf16[256,2048]{1,0:T(8,128)(2,1)} %get-tuple-element.8) | data formatting | bytes 2097152
  139.3 0.0 copy-done
  139.3 0.7 copy.14
Async XLA Ops:
  136.9 2.4 %copy-start = (f32[4,128,128]{2,1,0:T(8,128)S(1)}, f32[4,128,128]{2,1,0:T(8,128)}, u32[]{:S(2)}) copy-start(f32[4,128,128]{2,1,0:T(8,128)} %get-tuple-element.5) | copy-start | bytes 786436
